TPU v7x, 32 devices: a whole 2x2x4 slice. The times are simulated.
32 devices in a mesh: hours: 2 (over x), sta: 16 (over z, y, core).
Axes of the slice: x: 2, y: 2, z: 4, core: 2. Of those that a mesh axis runs over, the one named last changes fastest.
Arguments:
- spectra: bfloat16 [32, 32, 4, 2, 2048], P(('hours', 'sta')), parts along dimension 0, may hold values from -60 to 60
- station_counts: int32 [32], P(('hours', 'sta')), parts along dimension 0, may hold values from 16 to 32
- block_pairs: int32 [32, 2], P(('hours', 'sta')), parts along dimension 0, may hold values from 0 to 15, as said below
Outputs:
- correlations: bfloat16 [32, 32, 32, 512], P(('hours', 'sta')), parts along dimension 0
There are 2 independent parts, one for each index of `hours`. A program takes and returns all parts, laid end to end along the dimension named above; each array names one. Nothing has to cross between parts.
Inputs may be any that keep to these rules, and one draw needn't show every extreme that they name: Pair p's row block is held by the device that holds pair p: block_pairs[p, 0] == p; the column block's device, block_pairs[p, 1], differs from it by at most 3, and by exactly 3 for some pairs.
All inputs are finite; a program needn't handle non-finite values.
Results may differ from a plain program's by a relative error of at most 0.0065.
Values may be sent and summed in bfloat16 or wider, within the bound.
A program may use at most 192 MiB of HBM per device.

v0:
```python
import math

import jax
import jax.numpy as jnp
from jax import lax
from jax.sharding import PartitionSpec as P

LAGS = 512
BAND = 32
REACH = 3


EPSILON = 1e-06


def shifted(x, axis, by):
    peers = lax.axis_size(axis)
    pairs = [(i, i + by) for i in range(peers) if 0 <= i + by < peers]
    return lax.ppermute(x, axis, pairs)


def whiten(spectra, station_counts):
    values = spectra.astype(jnp.float32)
    blocks = values.shape[0]
    stations = values.shape[1]
    windows = values.shape[2]
    freqs = values.shape[4]
    power_sum = jnp.sum(values * values, axis=3)
    banded = power_sum.reshape(blocks, stations, windows, freqs // BAND, BAND)
    band_mean = jnp.mean(banded, axis=(2, 4))
    inverse_amp = jnp.repeat(lax.rsqrt(band_mean + EPSILON), BAND, axis=2)
    station_mask = (
        jnp.arange(stations, dtype=jnp.int32)[None, :] < station_counts[:, None]
    ).astype(jnp.float32)
    weights = inverse_amp * station_mask[:, :, None]
    return (values * weights[:, :, None, None, :]).astype(jnp.bfloat16)


def cross_spectra(first_block, other_block):
    left_real = first_block[..., 0, :]
    left_imag = first_block[..., 1, :]
    right_real = other_block[..., 0, :]
    right_imag = other_block[..., 1, :]
    stacked_left = jnp.concatenate([left_real, left_imag], axis=-2)
    real_right = jnp.concatenate([right_real, right_imag], axis=-2)
    imag_right = jnp.concatenate([-right_imag, right_real], axis=-2)
    real_part = jnp.einsum(
        "...iwf,...jwf->...ijf", stacked_left, real_right, preferred_element_type=jnp.float32
    )
    imag_part = jnp.einsum(
        "...iwf,...jwf->...ijf", stacked_left, imag_right, preferred_element_type=jnp.float32
    )
    return jnp.stack([real_part, imag_part], axis=-2).astype(jnp.bfloat16)


def lag_table(freqs, lags):
    freq_bins = jnp.arange(freqs, dtype=jnp.int32)
    lag_index = jnp.arange(lags, dtype=jnp.int32) - lags // 2
    phase_index = jnp.mod(freq_bins[:, None] * lag_index[None, :], 2 * freqs)
    angles = math.pi / freqs * phase_index.astype(jnp.float32)
    return jnp.concatenate([jnp.cos(angles), -jnp.sin(angles)], axis=0).astype(jnp.bfloat16)


def to_lags(crossed, dft_rows, windows):
    leading = crossed.shape[:-2]
    freqs = crossed.shape[-1]
    flat_rows = crossed.reshape(-1, 2 * freqs)
    summed = jnp.dot(flat_rows, dft_rows, preferred_element_type=jnp.float32)
    scaled = summed * (1.0 / math.sqrt(freqs * windows))
    return scaled.reshape(leading + (dft_rows.shape[1],)).astype(jnp.bfloat16)


def local(spectra, station_counts, block_pairs):
    whitened = whiten(spectra, station_counts)
    per_device = whitened.shape[0]
    windows = whitened.shape[2]
    freqs = whitened.shape[4]
    position = lax.axis_index("sta")
    pieces = []
    for offset in range(-REACH, REACH + 1):
        if offset == 0:
            pieces.append(whitened)
        else:
            pieces.append(shifted(whitened, "sta", -offset))
    neighbourhood = jnp.concatenate(pieces, axis=0)
    own_rows = block_pairs[:, 0] - position * per_device
    near_rows = block_pairs[:, 1] - (position - REACH) * per_device
    crossed = cross_spectra(
        jnp.take(whitened, own_rows, axis=0), jnp.take(neighbourhood, near_rows, axis=0)
    )
    return to_lags(crossed, lag_table(freqs, LAGS), windows)


def solution(mesh):
    placed = (
        P(("hours", "sta"), None, None, None, None),
        P(("hours", "sta")),
        P(("hours", "sta"), None),
    )
    return jax.shard_map(
        local,
        mesh=mesh,
        in_specs=placed,
        out_specs=P(("hours", "sta"), None, None, None),
        check_vma=False,
    )
```

profile of v0, /device:TPU:16, one launch (start us, length us, event | category | flops | bytes accessed | tf_op | source)
XLA Modules:
  0.0 231.8 jit_solution(5647925459087477511)
XLA Ops:
  0.0 0.0 copy-start.1
  0.0 1.3 fusion.17
  2.0 1.8 fusion.10
  3.8 0.3 copy.76
  4.1 0.2 bitcast_reduce_fusion
  4.3 0.1 copy.77
  4.4 0.3 broadcast_in_dim.35
  4.8 0.5 broadcast_in_dim.36
  5.9 0.1 broadcast_multiply_fusion
  6.0 0.0 copy-done.1
  6.0 0.7 broadcast_select_fusion
  6.7 2.9 %collective-permute-start = (bf16[1,32,4,2,2048]{4,1,3,2,0:T(8,128)(2,1)S(1)}, bf16[1,32,4,2,2048]{4,1,3,2,0:T(8,128)(2,1)}, u32[]{:S(2)}, u32[]{:S(2)}) collective-permute-start(bf16[1,32,4,2,2048]{4,1,3,2,0:T(8,128)(2,1)S(1)} %get-tuple-element.17), channel_id=1, source_target_pairs={{0,3},{1,4},{2,5},{3,6},{4,7},{5,8},{6,9},{7,10},{8,11},{9,12},{10... | collective-permute-start | bytes 3145736 | tf_op jit(solution)/shard_map/ppermute | solution.py:19
  9.6 3.4 %collective-permute-start.1 = (bf16[1,32,4,2,2048]{4,1,3,2,0:T(8,128)(2,1)S(1)}, bf16[1,32,4,2,2048]{4,1,3,2,0:T(8,128)(2,1)}, u32[]{:S(2)}, u32[]{:S(2)}) collective-permute-start(bf16[1,32,4,2,2048]{4,1,3,2,0:T(8,128)(2,1)S(1)} %get-tuple-element.17), channel_id=1, source_target_pairs={{0,2},{1,3},{2,4},{3,5},{4,6},{5,7},{6,8},{7,9},{8,10},{9,11},{10,... | collective-permute-start | bytes 3145736 | tf_op jit(solution)/shard_map/ppermute | solution.py:19
  13.0 2.4 %collective-permute-start.2 = (bf16[1,32,4,2,2048]{4,1,3,2,0:T(8,128)(2,1)S(1)}, bf16[1,32,4,2,2048]{4,1,3,2,0:T(8,128)(2,1)}, u32[]{:S(2)}, u32[]{:S(2)}) collective-permute-start(bf16[1,32,4,2,2048]{4,1,3,2,0:T(8,128)(2,1)S(1)} %get-tuple-element.17), channel_id=1, source_target_pairs={{0,1},{1,2},{2,3},{3,4},{4,5},{5,6},{6,7},{7,8},{8,9},{9,10},{10,1... | collective-permute-start | bytes 3145736 | tf_op jit(solution)/shard_map/ppermute | solution.py:19
  15.4 4.1 %collective-permute-start.3 = (bf16[1,32,4,2,2048]{4,1,3,2,0:T(8,128)(2,1)S(1)}, bf16[1,32,4,2,2048]{4,1,3,2,0:T(8,128)(2,1)}, u32[]{:S(2)}, u32[]{:S(2)}) collective-permute-start(bf16[1,32,4,2,2048]{4,1,3,2,0:T(8,128)(2,1)S(1)} %get-tuple-element.17), channel_id=1, source_target_pairs={{1,0},{2,1},{3,2},{4,3},{5,4},{6,5},{7,6},{8,7},{9,8},{10,9},{11,1... | collective-permute-start | bytes 3145736 | tf_op jit(solution)/shard_map/ppermute | solution.py:19
  19.5 2.4 %collective-permute-start.4 = (bf16[1,32,4,2,2048]{4,1,3,2,0:T(8,128)(2,1)S(1)}, bf16[1,32,4,2,2048]{4,1,3,2,0:T(8,128)(2,1)S(1)}, u32[]{:S(2)}, u32[]{:S(2)}) collective-permute-start(bf16[1,32,4,2,2048]{4,1,3,2,0:T(8,128)(2,1)S(1)} %get-tuple-element.17), channel_id=1, source_target_pairs={{2,0},{3,1},{4,2},{5,3},{6,4},{7,5},{8,6},{9,7},{10,8},{11,9},{12,... | collective-permute-start | bytes 3145736 | tf_op jit(solution)/shard_map/ppermute | solution.py:19
  21.9 18.2 %cosine_convert_fusion = (bf16[2048,512]{1,0:T(8,128)(2,1)}, bf16[2048,512]{1,0:T(8,128)(2,1)}) fusion(s32[512]{0:T(512)S(1)} %iota_add_fusion), kind=kLoop, calls=%fused_computation.14 | loop fusion | flops 17825792 | bytes 4196352 | tf_op jit(solution)/shard_map/convert
  40.2 0.1 slice_bitcast_fusion.1
  40.2 0.1 maximum_bitcast_fusion.1
  41.0 4.2 %copy.71 = bf16[32,8,2048]{0,1,2:T(8,128)(2,1)} copy(bf16[32,8,2048]{2,0,1:T(8,128)(2,1)S(1)} %maximum_bitcast_fusion.1) | data formatting | bytes 2097152 | tf_op jit(solution)/shard_map/reshape.13
  45.2 29.6 %collective-permute-done = bf16[1,32,4,2,2048]{4,1,3,2,0:T(8,128)(2,1)} collective-permute-done((bf16[1,32,4,2,2048]{4,1,3,2,0:T(8,128)(2,1)S(1)}, bf16[1,32,4,2,2048]{4,1,3,2,0:T(8,128)(2,1)}, u32[]{:S(2)}, u32[]{:S(2)}) %collective-permute-start) | collective-permute-done | bytes 1048608 | tf_op jit(solution)/shard_map/ppermute | solution.py:19
  74.8 2.1 collective-permute-start.5
  76.9 1.3 constant_dynamic-update-slice_fusion.6
  78.2 19.1 %collective-permute-done.1 = bf16[1,32,4,2,2048]{4,1,3,2,0:T(8,128)(2,1)} collective-permute-done((bf16[1,32,4,2,2048]{4,1,3,2,0:T(8,128)(2,1)S(1)}, bf16[1,32,4,2,2048]{4,1,3,2,0:T(8,128)(2,1)}, u32[]{:S(2)}, u32[]{:S(2)}) %collective-permute-start.1) | collective-permute-done | bytes 1048608 | tf_op jit(solution)/shard_map/ppermute | solution.py:19
  97.3 1.3 constant_dynamic-update-slice_fusion.5
  98.6 0.0 collective-permute-done.2
  98.6 1.3 constant_dynamic-update-slice_fusion.4
  99.9 0.1 constant_dynamic-update-slice_fusion.3
  100.0 0.0 collective-permute-done.3
  100.0 1.3 constant_dynamic-update-slice_fusion.2
  101.3 4.9 %collective-permute-done.4 = bf16[1,32,4,2,2048]{4,1,3,2,0:T(8,128)(2,1)S(1)} collective-permute-done((bf16[1,32,4,2,2048]{4,1,3,2,0:T(8,128)(2,1)S(1)}, bf16[1,32,4,2,2048]{4,1,3,2,0:T(8,128)(2,1)S(1)}, u32[]{:S(2)}, u32[]{:S(2)}) %collective-permute-start.4) | collective-permute-done | bytes 1048608 | tf_op jit(solution)/shard_map/ppermute | solution.py:19
  106.2 0.1 constant_dynamic-update-slice_fusion.1
  106.3 0.6 collective-permute-done.5
  106.9 0.1 constant_dynamic-update-slice_fusion
  107.1 0.1 dynamic-slice_select_fusion
  107.2 0.1 slice_bitcast_fusion.2
  107.3 0.2 maximum_bitcast_fusion
  107.5 4.3 %copy.70 = bf16[32,8,2048]{0,1,2:T(8,128)(2,1)} copy(bf16[32,8,2048]{2,0,1:T(8,128)(2,1)S(1)} %get-tuple-element.22) | data formatting | bytes 2097152 | tf_op jit(solution)/shard_map/reshape.12
  111.8 4.2 %copy.72 = bf16[32,8,2048]{0,1,2:T(8,128)(2,1)} copy(bf16[32,8,2048]{2,0,1:T(8,128)(2,1)S(1)} %get-tuple-element.23) | data formatting | bytes 2097152 | tf_op jit(solution)/shard_map/reshape.15
  116.0 11.0 %convert_bitcast_fusion.1 = bf16[1,32,32,1,2048]{1,2,4,3,0:T(8,128)(2,1)} fusion(bf16[32,8,2048]{0,1,2:T(8,128)(2,1)} %copy.70, bf16[32,8,2048]{0,1,2:T(8,128)(2,1)} %copy.71), kind=kOutput, calls=%fused_computation.2 | convolution fusion | flops 35651584 | bytes 6291456 | tf_op jit(solution)/shard_map/...iwf,...jwf->...ijf/dot_general | solution.py:47
  127.0 0.0 copy-done
  127.0 9.5 %convert_bitcast_fusion = bf16[1,32,32,1,2048]{1,2,4,3,0:T(8,128)(2,1)} fusion(bf16[32,8,2048]{0,1,2:T(8,128)(2,1)} %copy.72, bf16[32,8,2048]{0,1,2:T(8,128)(2,1)S(1)} %copy-done), kind=kOutput, calls=%fused_computation.1 | convolution fusion | flops 35651584 | bytes 6291456 | tf_op jit(solution)/shard_map/...iwf,...jwf->...ijf/dot_general | solution.py:50
  136.5 22.7 %pad_maximum_fusion = bf16[1,32,32,2,2048]{1,2,4,3,0:T(8,128)(2,1)} fusion(bf16[1,32,32,1,2048]{1,2,4,3,0:T(8,128)(2,1)} %convert_bitcast_fusion, bf16[1,32,32,1,2048]{1,2,4,3,0:T(8,128)(2,1)} %convert_bitcast_fusion.1), kind=kLoop, calls=%fused_computation | loop fusion | flops 4194304 | bytes 16777216 | tf_op jit(solution)/shard_map/stack | solution.py:53
  159.2 51.6 %copy.74 = bf16[1,32,32,2,2048]{4,3,2,1,0:T(2,128)(2,1)} copy(bf16[1,32,32,2,2048]{1,2,4,3,0:T(8,128)(2,1)} %pad_maximum_fusion) | data formatting | bytes 16777216 | tf_op jit(solution)/shard_map/stack | solution.py:53
  210.8 12.2 %copy.80 = bf16[128,8,2,2048]{3,1,2,0:T(8,128)(2,1)} copy(bf16[128,8,2,2048]{3,2,1,0:T(2,128)(2,1)} %bitcast.52) | data formatting | bytes 16777216
  223.0 0.0 copy-done.2
  223.0 0.0 copy-done.3
  223.0 8.8 %multiply_convert_fusion = bf16[1024,512]{1,0:T(8,128)(2,1)} fusion(bf16[1024,4096]{1,0:T(8,128)(2,1)} %bitcast.53, bf16[2048,512]{1,0:T(8,128)(2,1)S(1)} %copy-done.3, bf16[2048,512]{1,0:T(8,128)(2,1)S(1)} %copy-done.2), kind=kOutput, calls=%fused_computation.22 | convolution fusion | flops 4304404480 | bytes 13631488 | tf_op jit(solution)/shard_map/dot_general | solution.py:68
  (7 shorter events, 0.1 us)
Async XLA Ops:
  0.0 6.0 %copy-start.1 = (bf16[1,32,4,2,2048]{4,3,2,1,0:T(2,128)(2,1)S(1)}, bf16[1,32,4,2,2048]{4,3,2,1,0:T(2,128)(2,1)}, u32[]{:S(2)}) copy-start(bf16[1,32,4,2,2048]{4,3,2,1,0:T(2,128)(2,1)} %param.3) | copy-start | bytes 3145732
  6.7 68.1 %collective-permute-start = (bf16[1,32,4,2,2048]{4,1,3,2,0:T(8,128)(2,1)S(1)}, bf16[1,32,4,2,2048]{4,1,3,2,0:T(8,128)(2,1)}, u32[]{:S(2)}, u32[]{:S(2)}) collective-permute-start(bf16[1,32,4,2,2048]{4,1,3,2,0:T(8,128)(2,1)S(1)} %get-tuple-element.17), channel_id=1, source_target_pairs={{0,3},{1,4},{2,5},{3,6},{4,7},{5,8},{6,9},{7,10},{8,11},{9,12},{10... | collective-permute-start | bytes 3145736 | tf_op jit(solution)/shard_map/ppermute | solution.py:19
  9.6 87.7 %collective-permute-start.1 = (bf16[1,32,4,2,2048]{4,1,3,2,0:T(8,128)(2,1)S(1)}, bf16[1,32,4,2,2048]{4,1,3,2,0:T(8,128)(2,1)}, u32[]{:S(2)}, u32[]{:S(2)}) collective-permute-start(bf16[1,32,4,2,2048]{4,1,3,2,0:T(8,128)(2,1)S(1)} %get-tuple-element.17), channel_id=1, source_target_pairs={{0,2},{1,3},{2,4},{3,5},{4,6},{5,7},{6,8},{7,9},{8,10},{9,11},{10,... | collective-permute-start | bytes 3145736 | tf_op jit(solution)/shard_map/ppermute | solution.py:19
  13.0 85.5 %collective-permute-start.2 = (bf16[1,32,4,2,2048]{4,1,3,2,0:T(8,128)(2,1)S(1)}, bf16[1,32,4,2,2048]{4,1,3,2,0:T(8,128)(2,1)}, u32[]{:S(2)}, u32[]{:S(2)}) collective-permute-start(bf16[1,32,4,2,2048]{4,1,3,2,0:T(8,128)(2,1)S(1)} %get-tuple-element.17), channel_id=1, source_target_pairs={{0,1},{1,2},{2,3},{3,4},{4,5},{5,6},{6,7},{7,8},{8,9},{9,10},{10,1... | collective-permute-start | bytes 3145736 | tf_op jit(solution)/shard_map/ppermute | solution.py:19
  15.4 84.6 %collective-permute-start.3 = (bf16[1,32,4,2,2048]{4,1,3,2,0:T(8,128)(2,1)S(1)}, bf16[1,32,4,2,2048]{4,1,3,2,0:T(8,128)(2,1)}, u32[]{:S(2)}, u32[]{:S(2)}) collective-permute-start(bf16[1,32,4,2,2048]{4,1,3,2,0:T(8,128)(2,1)S(1)} %get-tuple-element.17), channel_id=1, source_target_pairs={{1,0},{2,1},{3,2},{4,3},{5,4},{6,5},{7,6},{8,7},{9,8},{10,9},{11,1... | collective-permute-start | bytes 3145736 | tf_op jit(solution)/shard_map/ppermute | solution.py:19
  19.5 86.7 %collective-permute-start.4 = (bf16[1,32,4,2,2048]{4,1,3,2,0:T(8,128)(2,1)S(1)}, bf16[1,32,4,2,2048]{4,1,3,2,0:T(8,128)(2,1)S(1)}, u32[]{:S(2)}, u32[]{:S(2)}) collective-permute-start(bf16[1,32,4,2,2048]{4,1,3,2,0:T(8,128)(2,1)S(1)} %get-tuple-element.17), channel_id=1, source_target_pairs={{2,0},{3,1},{4,2},{5,3},{6,4},{7,5},{8,6},{9,7},{10,8},{11,9},{12,... | collective-permute-start | bytes 3145736 | tf_op jit(solution)/shard_map/ppermute | solution.py:19
  74.8 32.1 %collective-permute-start.5 = (bf16[1,32,4,2,2048]{4,1,3,2,0:T(8,128)(2,1)S(1)}, bf16[1,32,4,2,2048]{4,1,3,2,0:T(8,128)(2,1)S(1)}, u32[]{:S(2)}, u32[]{:S(2)}) collective-permute-start(bf16[1,32,4,2,2048]{4,1,3,2,0:T(8,128)(2,1)S(1)} %get-tuple-element.17), channel_id=1, source_target_pairs={{3,0},{4,1},{5,2},{6,3},{7,4},{8,5},{9,6},{10,7},{11,8},{12,9},{13... | collective-permute-start | bytes 3145736 | tf_op jit(solution)/shard_map/ppermute | solution.py:19
  116.0 11.0 %copy-start = (bf16[32,8,2048]{0,1,2:T(8,128)(2,1)S(1)}, bf16[32,8,2048]{0,1,2:T(8,128)(2,1)}, u32[]{:S(2)}) copy-start(bf16[32,8,2048]{0,1,2:T(8,128)(2,1)} %copy.71) | copy-start | bytes 3145732
  210.8 12.2 %copy-start.2 = (bf16[2048,512]{1,0:T(8,128)(2,1)S(1)}, bf16[2048,512]{1,0:T(8,128)(2,1)}, u32[]{:S(2)}) copy-start(bf16[2048,512]{1,0:T(8,128)(2,1)} %get-tuple-element.24) | copy-start | bytes 6291460
  210.8 12.2 %copy-start.3 = (bf16[2048,512]{1,0:T(8,128)(2,1)S(1)}, bf16[2048,512]{1,0:T(8,128)(2,1)}, u32[]{:S(2)}) copy-start(bf16[2048,512]{1,0:T(8,128)(2,1)} %get-tuple-element.25) | copy-start | bytes 6291460
where the time goes:
time: 234 us; the launch traced here: 232 us
  local copies, waits for them, and re-layouts  84.7 us (36%)
  waiting for transfers between devices  54.2 us (23%)
  other arithmetic  44.2 us (19%)
  matrix products  29.3 us (13%)
  starting transfers between devices  17.3 us (7%)
    ppermute x6, waiting for transfers between devices, shifted(): return lax.ppermute(x, axis, pairs)  54.2 us
    another operation x1, local copies, waits for them, and re-layouts, cross_spectra(): return jnp.stack([real_part, imag_part], axis=-2).astype(jnp.bfloat16)  51.6 us
    another operation x1, other arithmetic, cross_spectra(): return jnp.stack([real_part, imag_part], axis=-2).astype(jnp.bfloat16)  22.7 us
    another operation x3, other arithmetic  18.5 us
    unnamed x17, local copies, waits for them, and re-layouts  18 us
    ppermute x6, starting transfers between devices, shifted(): return lax.ppermute(x, axis, pairs)  17.3 us
    another operation x3, local copies, waits for them, and re-layouts  12.7 us
    dot_general x1, matrix products, cross_spectra(): jnp.einsum('...iwf,...jwf->...ijf', stacked_left, real_right, preferred_e...  11 us
  transfers between devices with their start and end apart: 6, of which 4 were waited for; matrix products, arithmetic and copies ran while one was open for 12% of the time, Pallas kernels for 0%

commit v1 on v0

v1 whole, which is shorter than its diff:
```python
import functools
import math

import jax
import jax.numpy as jnp
from jax import lax
from jax.experimental import pallas as pl
from jax.experimental.pallas import tpu as pltpu
from jax.sharding import PartitionSpec as P

LAGS = 512
BAND = 32
EPSILON = 1e-06
CHUNK = 256
HALF = LAGS // 2

SIB, MIR, DIAG, SIBMIR, VERT, SIBVERT, OWN = range(7)


def kernel(sta, windows, freqs, counts, pairs, x_ref, out_ref, held, left, right, rows_re, rows_im,
           base, table, acc, sends, recvs):
    chunks = freqs // CHUNK
    parts = 2 * windows
    me = lax.axis_index("sta")
    planes = sta // 4
    plane = me // 4
    odd = lax.rem(me, 2)
    upper = lax.rem(me // 2, 2)
    spot = lax.rem(me, 4)
    inner = jnp.logical_or(spot == 1, spot == 2)
    below = plane > 0
    above = plane < planes - 1
    sibling = me + 1 - 2 * odd
    mirror = me + 2 - 4 * upper
    cross_mirror = me + 3 - 2 * spot
    diag = me - 3 + 6 * odd
    has_diag = jnp.where(odd == 1, above, below)
    up_vert = me + 4 - 8 * upper
    has_up = jnp.where(upper == 1, below, above)
    down_vert = me - 4 + 8 * upper
    has_down = jnp.where(upper == 1, above, below)

    barrier = pltpu.get_barrier_semaphore()

    def greet(other):
        pl.semaphore_signal(barrier, inc=1, device_id={"sta": other}, device_id_type=pl.DeviceIdType.MESH)

    greet(sibling)
    greet(mirror)
    greet(cross_mirror)
    pl.when(has_diag)(lambda: greet(diag))
    pl.when(has_up)(lambda: greet(up_vert))
    pl.when(has_down)(lambda: greet(down_vert))

    def copy(n, source, target, other, number):
        return pltpu.make_async_remote_copy(
            src_ref=held.at[n, source], dst_ref=held.at[n, target],
            send_sem=sends.at[n, number], recv_sem=recvs.at[n, target],
            device_id={"sta": other}, device_id_type=pl.DeviceIdType.MESH)

    def to_sib(n):
        return copy(n, OWN, SIB, sibling, 0)

    def to_mir(n):
        return copy(n, OWN, MIR, mirror, 1)

    def to_diag(n):
        return copy(n, OWN, DIAG, diag, 2)

    def mir_to_sib(n):
        return copy(n, MIR, SIBMIR, sibling, 3)

    def mir_to_vert(n):
        return copy(n, MIR, VERT, up_vert, 4)

    def vert_to_sib(n):
        return copy(n, VERT, SIBVERT, sibling, 5)

    def diag_to_mir(n):
        return copy(n, DIAG, VERT, cross_mirror, 6)

    def turned(n):
        return jnp.logical_and(inner, lax.rem(n, 2) == 1)

    def sends_vert(n):
        return jnp.logical_and(has_up, jnp.logical_not(turned(n)))

    def sends_turned(n):
        return jnp.logical_and(has_diag, turned(n))

    count = counts[0]
    station = lax.broadcasted_iota(jnp.int32, (32, CHUNK), 0)
    mask = jnp.where(station < count, 1.0, 0.0).astype(jnp.float32)
    band_row = lax.broadcasted_iota(jnp.int32, (CHUNK, CHUNK), 0)
    band_col = lax.broadcasted_iota(jnp.int32, (CHUNK, CHUNK), 1)
    same_band = jnp.where(
        jnp.right_shift(band_row, 5) == jnp.right_shift(band_col, 5), 1.0 / (BAND * windows), 0.0
    ).astype(jnp.float32)

    def whiten(n):
        cols = pl.ds(pl.multiple_of(n * CHUNK, CHUNK), CHUNK)
        power = jnp.zeros((32, CHUNK), jnp.float32)
        for part in range(parts):
            value = x_ref[part, :, cols].astype(jnp.float32)
            power += value * value
        mean = jnp.dot(power, same_band, precision=lax.Precision.HIGHEST, preferred_element_type=jnp.float32)
        weight = lax.rsqrt(mean + EPSILON) * mask
        for part in range(parts):
            value = x_ref[part, :, cols].astype(jnp.float32)
            held[n, OWN, part] = (value * weight).astype(jnp.bfloat16)

    def start_own(n):
        whiten(n)
        to_mir(n).start()
        pl.when(has_diag)(lambda: to_diag(n).start())
        to_sib(n).start()

    whiten(0)
    pl.semaphore_wait(
        barrier, 3 + has_diag.astype(jnp.int32) + has_up.astype(jnp.int32) + has_down.astype(jnp.int32))
    to_mir(0).start()
    pl.when(has_diag)(lambda: to_diag(0).start())
    to_sib(0).start()
    start_own(1)
    start_own(2)

    def angle_of(phase):
        period = 4 * freqs
        phase = jnp.bitwise_and(phase, period - 1)
        phase = jnp.where(phase >= period // 2, phase - period, phase)
        return (math.pi / (2 * freqs)) * phase.astype(jnp.float32)

    base_angle = angle_of(band_row * (2 * band_col + 1))
    base[0] = jnp.cos(base_angle)
    base[1] = jnp.sin(base_angle)
    acc[...] = jnp.zeros_like(acc)

    wanted = pairs[0, 1]
    found = {SIB: sibling, MIR: mirror, DIAG: diag, SIBMIR: cross_mirror,
             VERT: me - 2 + 4 * upper, SIBVERT: sibling - 2 + 4 * upper}

    def compute(n):
        lag = lax.broadcasted_iota(jnp.int32, (1, HALF), 1)
        step = angle_of(n * CHUNK * (2 * lag + 1))
        step_cos, step_sin = jnp.cos(step), jnp.sin(step)
        table[0] = (base[0] * step_cos - base[1] * step_sin).astype(jnp.bfloat16)
        table[1] = (base[1] * step_cos + base[0] * step_sin).astype(jnp.bfloat16)
        freq = n * CHUNK + lax.broadcasted_iota(jnp.int32, (1, CHUNK), 1)
        turn = angle_of(freq)
        turn_cos, turn_sin = jnp.cos(turn), jnp.sin(turn)
        for w in range(windows):
            real = held[n, OWN, 2 * w].astype(jnp.float32)
            imag = held[n, OWN, 2 * w + 1].astype(jnp.float32)
            left[2 * w] = real * turn_cos + imag * turn_sin
            left[2 * w + 1] = imag * turn_cos - real * turn_sin
        for part in range(parts):
            value = held[n, OWN, part]
            for kind, block in found.items():
                value = jnp.where(wanted == block, held[n, kind, part], value)
            right[part] = value.astype(jnp.float32)

        def some_rows(g, carry):
            for u in range(8):
                i = g * 8 + u
                re = jnp.zeros((32, CHUNK), jnp.float32)
                im = jnp.zeros((32, CHUNK), jnp.float32)
                for w in range(windows):
                    lr = left[2 * w, pl.ds(i, 1), :]
                    li = left[2 * w + 1, pl.ds(i, 1), :]
                    rr = right[2 * w]
                    ri = right[2 * w + 1]
                    re += lr * rr + li * ri
                    im += li * rr - lr * ri
                rows_re[u * 32:(u + 1) * 32] = re.astype(jnp.bfloat16)
                rows_im[u * 32:(u + 1) * 32] = im.astype(jnp.bfloat16)
            where = pl.ds(pl.multiple_of(g * 256, 256), 256)
            acc[0, where] += jnp.dot(rows_re[...], table[0], preferred_element_type=jnp.float32)
            acc[1, where] += jnp.dot(rows_im[...], table[1], preferred_element_type=jnp.float32)
            return carry

        lax.fori_loop(0, 4, some_rows, 0)

    def vert_arrives(n):
        return jnp.where(turned(n), has_down, has_down)

    def one_step(n, carry):
        @pl.when(n < chunks)
        def _():
            to_mir(n).wait_recv()
            pl.when(sends_vert(n))(lambda: mir_to_vert(n).start())
            mir_to_sib(n).start()
            pl.when(has_diag)(lambda: to_diag(n).wait_recv())
            pl.when(sends_turned(n))(lambda: diag_to_mir(n).start())

        @pl.when(n + 3 < chunks)
        def _():
            start_own(n + 3)

        @pl.when(jnp.logical_and(n >= 1, n <= chunks))
        def _():
            @pl.when(has_down)
            def _():
                mir_to_vert(n - 1).wait_recv()
                vert_to_sib(n - 1).start()

        @pl.when(n >= 2)
        def _():
            m = n - 2
            to_sib(m).wait_recv()
            mir_to_sib(m).wait_recv()
            pl.when(has_down)(lambda: vert_to_sib(m).wait_recv())
            compute(m)
        return carry

    lax.fori_loop(0, chunks + 2, one_step, 0)

    def finish(n, carry):
        to_sib(n).wait_send()
        to_mir(n).wait_send()
        pl.when(has_diag)(lambda: to_diag(n).wait_send())
        mir_to_sib(n).wait_send()
        pl.when(sends_vert(n))(lambda: mir_to_vert(n).wait_send())
        pl.when(has_down)(lambda: vert_to_sib(n).wait_send())
        pl.when(sends_turned(n))(lambda: diag_to_mir(n).wait_send())
        return carry

    lax.fori_loop(0, chunks, finish, 0)

    scale = 1.0 / math.sqrt(freqs * windows)
    flip = jnp.where(band_row + band_col == HALF - 1, 1.0, 0.0).astype(jnp.bfloat16)

    def write(g, carry):
        where = pl.ds(pl.multiple_of(g * 256, 256), 256)
        even, odd_part = acc[0, where], acc[1, where]
        out_ref[where, HALF:] = ((even - odd_part) * scale).astype(jnp.bfloat16)
        mirrored = ((even + odd_part) * scale).astype(jnp.bfloat16)
        out_ref[where, :HALF] = jnp.dot(mirrored, flip, preferred_element_type=jnp.float32).astype(jnp.bfloat16)
        return carry

    lax.fori_loop(0, 4, write, 0)


def local(sta, spectra, station_counts, block_pairs):
    _, stations, windows, two, freqs = spectra.shape
    chunks = freqs // CHUNK
    parts = two * windows
    arranged = jnp.transpose(spectra.reshape(stations, parts, freqs), (1, 0, 2))
    out = pl.pallas_call(
        functools.partial(kernel, sta, windows, freqs),
        out_shape=jax.ShapeDtypeStruct((stations * stations, LAGS), jnp.bfloat16),
        in_specs=[
            pl.BlockSpec(memory_space=pltpu.SMEM),
            pl.BlockSpec(memory_space=pltpu.SMEM),
            pl.BlockSpec(memory_space=pltpu.VMEM),
        ],
        out_specs=pl.BlockSpec(memory_space=pltpu.VMEM),
        scratch_shapes=[
            pltpu.VMEM((chunks, 7, parts, stations, CHUNK), jnp.bfloat16),
            pltpu.VMEM((parts, stations, CHUNK), jnp.float32),
            pltpu.VMEM((parts, stations, CHUNK), jnp.float32),
            pltpu.VMEM((256, CHUNK), jnp.bfloat16),
            pltpu.VMEM((256, CHUNK), jnp.bfloat16),
            pltpu.VMEM((2, CHUNK, HALF), jnp.float32),
            pltpu.VMEM((2, CHUNK, HALF), jnp.bfloat16),
            pltpu.VMEM((2, stations * stations, HALF), jnp.float32),
            pltpu.SemaphoreType.DMA((chunks, 7)),
            pltpu.SemaphoreType.DMA((chunks, 6)),
        ],
        compiler_params=pltpu.CompilerParams(
            collective_id=0, has_side_effects=True, vmem_limit_bytes=40 * 1024 * 1024),
    )(station_counts, block_pairs, arranged)
    return out.reshape(1, stations, stations, LAGS)


def solution(mesh):
    placed = (
        P(("hours", "sta"), None, None, None, None),
        P(("hours", "sta")),
        P(("hours", "sta"), None),
    )
    return jax.shard_map(
        functools.partial(local, mesh.shape["sta"]),
        mesh=mesh,
        in_specs=placed,
        out_specs=P(("hours", "sta"), None, None, None),
        check_vma=False,
    )
```

time: 234 us -> 48.2 us (0.21)
  the two profiles are of different devices: /device:TPU:16 before, /device:TPU:9 now
where the time goes in v1:
time: 48.2 us; the launch traced here: 48.1 us
  Pallas kernels  44 us (91%)
  local copies, waits for them, and re-layouts  3.43 us (7%)
  between operations  0.67 us (1%)
    pallas_call x1, Pallas kernels, local(): pl.pallas_call(functools.partial(kernel, sta, windows, freqs), out_shape=...  44 us
    unnamed x4, local copies, waits for them, and re-layouts  3.43 us

profile of v1, /device:TPU:9, one launch (start us, length us, event | category | flops | bytes accessed | tf_op | source)
XLA Modules:
  0.0 48.1 jit_solution(10302801093201787986)
XLA Ops:
  0.7 1.8 %copy.4 = bf16[1,32,4,2,2048]{4,1,3,2,0:T(8,128)(2,1)S(1)} copy(bf16[1,32,4,2,2048]{4,3,2,1,0:T(2,128)(2,1)} %param.3) | data formatting | bytes 2097152 | tf_op args[0]
  2.5 0.0 copy-start
  2.5 0.6 %copy-done = s32[1,2]{1,0:T(1,128)S(1)} copy-done((s32[1,2]{1,0:T(1,128)S(1)}, s32[1,2]{1,0:T(1,128)}, u32[]{:S(2)}) %copy-start) | copy-done | bytes 32
  3.1 44.0 %shard_map.37 = bf16[1024,512]{1,0:T(8,128)(2,1)S(1)} custom-call(s32[1]{0:T(128)S(6)} %copy.6.counts, s32[1,2]{1,0:T(1,128)S(1)} %copy-done, bf16[8,32,2048]{2,1,0:T(8,128)(2,1)S(1)} %bitcast.5), custom_call_target="tpu_custom_call" | custom-call | tf_op jit(solution)/shard_map/pallas_call | solution.py:248
  47.1 1.0 %copy.7 = bf16[1,32,32,512]{3,2,1,0:T(8,128)(2,1)} copy(bf16[1,32,32,512]{3,2,1,0:T(8,128)(2,1)S(1)} %bitcast.4) | data formatting | bytes 2097152
Async XLA Ops:
  2.5 0.7 %copy-start = (s32[1,2]{1,0:T(1,128)S(1)}, s32[1,2]{1,0:T(1,128)}, u32[]{:S(2)}) copy-start(s32[1,2]{1,0:T(1,128)} %pairs.1) | copy-start | bytes 28

commit v2 on v1

--- a/solution.py
+++ b/solution.py
@@ -12,13 +12,14 @@
 BAND = 32
 EPSILON = 1e-06
 CHUNK = 256
+AHEAD = 4
 HALF = LAGS // 2
 
-SIB, MIR, DIAG, SIBMIR, VERT, SIBVERT, OWN = range(7)
+SIB, MIR, DIAG, SIBMIR, VERT, PICK, OWN = range(7)
 
 
 def kernel(sta, windows, freqs, counts, pairs, x_ref, out_ref, held, left, right, rows_re, rows_im,
-           base, table, acc, sends, recvs):
+           base, table, acc, my_want, their_want, sends, recvs, want_sems):
     chunks = freqs // CHUNK
     parts = 2 * windows
     me = lax.axis_index("sta")
@@ -34,7 +35,9 @@
     mirror = me + 2 - 4 * upper
     cross_mirror = me + 3 - 2 * spot
     diag = me - 3 + 6 * odd
-    has_diag = jnp.where(odd == 1, above, below)
+    diag_out = jnp.logical_and(jnp.logical_not(inner), jnp.where(odd == 1, above, below))
+    diag_in = jnp.logical_and(inner, jnp.where(odd == 1, above, below))
+    has_diag = jnp.logical_or(diag_out, diag_in)
     up_vert = me + 4 - 8 * upper
     has_up = jnp.where(upper == 1, below, above)
     down_vert = me - 4 + 8 * upper
@@ -47,7 +50,6 @@
 
     greet(sibling)
     greet(mirror)
-    greet(cross_mirror)
     pl.when(has_diag)(lambda: greet(diag))
     pl.when(has_up)(lambda: greet(up_vert))
     pl.when(has_down)(lambda: greet(down_vert))
@@ -70,23 +72,13 @@
     def mir_to_sib(n):
         return copy(n, MIR, SIBMIR, sibling, 3)
 
-    def mir_to_vert(n):
-        return copy(n, MIR, VERT, up_vert, 4)
-
-    def vert_to_sib(n):
-        return copy(n, VERT, SIBVERT, sibling, 5)
-
-    def diag_to_mir(n):
-        return copy(n, DIAG, VERT, cross_mirror, 6)
-
-    def turned(n):
-        return jnp.logical_and(inner, lax.rem(n, 2) == 1)
-
-    def sends_vert(n):
-        return jnp.logical_and(has_up, jnp.logical_not(turned(n)))
-
-    def sends_turned(n):
-        return jnp.logical_and(has_diag, turned(n))
+    def pick_to_vert(n):
+        return copy(n, PICK, VERT, up_vert, 4)
+
+    def want_copy():
+        return pltpu.make_async_remote_copy(
+            src_ref=my_want, dst_ref=their_want, send_sem=want_sems.at[0], recv_sem=want_sems.at[1],
+            device_id={"sta": down_vert}, device_id_type=pl.DeviceIdType.MESH)
 
     count = counts[0]
     station = lax.broadcasted_iota(jnp.int32, (32, CHUNK), 0)
@@ -112,17 +104,20 @@
     def start_own(n):
         whiten(n)
         to_mir(n).start()
-        pl.when(has_diag)(lambda: to_diag(n).start())
+        pl.when(diag_out)(lambda: to_diag(n).start())
         to_sib(n).start()
 
+    wanted = pairs[0, 1]
+    my_want[...] = jnp.full_like(my_want, wanted.astype(jnp.float32))
     whiten(0)
     pl.semaphore_wait(
-        barrier, 3 + has_diag.astype(jnp.int32) + has_up.astype(jnp.int32) + has_down.astype(jnp.int32))
+        barrier, 2 + has_diag.astype(jnp.int32) + has_up.astype(jnp.int32) + has_down.astype(jnp.int32))
     to_mir(0).start()
-    pl.when(has_diag)(lambda: to_diag(0).start())
+    pl.when(diag_out)(lambda: to_diag(0).start())
     to_sib(0).start()
-    start_own(1)
-    start_own(2)
+    pl.when(has_down)(lambda: want_copy().start())
+    for n in range(1, AHEAD):
+        start_own(n)
 
     def angle_of(phase):
         period = 4 * freqs
@@ -135,9 +130,9 @@
     base[1] = jnp.sin(base_angle)
     acc[...] = jnp.zeros_like(acc)
 
-    wanted = pairs[0, 1]
-    found = {SIB: sibling, MIR: mirror, DIAG: diag, SIBMIR: cross_mirror,
-             VERT: me - 2 + 4 * upper, SIBVERT: sibling - 2 + 4 * upper}
+    from_vert = jnp.where(upper == 1, wanted >= 4 * plane + 4, wanted < 4 * plane)
+    found = ((SIB, wanted == sibling), (MIR, wanted == mirror), (SIBMIR, wanted == cross_mirror),
+             (DIAG, jnp.logical_and(inner, wanted == diag)), (VERT, from_vert))
 
     def compute(n):
         lag = lax.broadcasted_iota(jnp.int32, (1, HALF), 1)
@@ -155,8 +150,8 @@
             left[2 * w + 1] = imag * turn_cos - real * turn_sin
         for part in range(parts):
             value = held[n, OWN, part]
-            for kind, block in found.items():
-                value = jnp.where(wanted == block, held[n, kind, part], value)
+            for kind, is_it in found:
+                value = jnp.where(is_it, held[n, kind, part], value)
             right[part] = value.astype(jnp.float32)
 
         def some_rows(g, carry):
@@ -180,36 +175,42 @@
 
         lax.fori_loop(0, 4, some_rows, 0)
 
-    def vert_arrives(n):
-        return jnp.where(turned(n), has_down, has_down)
+    pl.when(has_up)(lambda: want_copy().wait_recv())
+    above_wants = jnp.max(their_want[...])
+    picks_mirror = above_wants == mirror.astype(jnp.float32)
+    picks_cross = above_wants == cross_mirror.astype(jnp.float32)
+
+    def pick(n):
+        for part in range(parts):
+            value = jnp.where(picks_mirror, held[n, MIR, part], held[n, SIB, part])
+            held[n, PICK, part] = jnp.where(picks_cross, held[n, SIBMIR, part], value)
 
     def one_step(n, carry):
         @pl.when(n < chunks)
         def _():
             to_mir(n).wait_recv()
-            pl.when(sends_vert(n))(lambda: mir_to_vert(n).start())
             mir_to_sib(n).start()
-            pl.when(has_diag)(lambda: to_diag(n).wait_recv())
-            pl.when(sends_turned(n))(lambda: diag_to_mir(n).start())
-
-        @pl.when(n + 3 < chunks)
-        def _():
-            start_own(n + 3)
-
-        @pl.when(jnp.logical_and(n >= 1, n <= chunks))
-        def _():
-            @pl.when(has_down)
+
+        @pl.when(n + AHEAD < chunks)
+        def _():
+            start_own(n + AHEAD)
+
+        @pl.when(n >= 2)
+        def _():
+            m = n - 2
+            pl.when(diag_in)(lambda: to_diag(m).wait_recv())
+            pl.when(has_down)(lambda: pick_to_vert(m).wait_recv())
+            compute(m)
+
+        @pl.when(n < chunks)
+        def _():
+            to_sib(n).wait_recv()
+            mir_to_sib(n).wait_recv()
+
+            @pl.when(has_up)
             def _():
-                mir_to_vert(n - 1).wait_recv()
-                vert_to_sib(n - 1).start()
-
-        @pl.when(n >= 2)
-        def _():
-            m = n - 2
-            to_sib(m).wait_recv()
-            mir_to_sib(m).wait_recv()
-            pl.when(has_down)(lambda: vert_to_sib(m).wait_recv())
-            compute(m)
+                pick(n)
+                pick_to_vert(n).start()
         return carry
 
     lax.fori_loop(0, chunks + 2, one_step, 0)
@@ -217,14 +218,13 @@
     def finish(n, carry):
         to_sib(n).wait_send()
         to_mir(n).wait_send()
-        pl.when(has_diag)(lambda: to_diag(n).wait_send())
+        pl.when(diag_out)(lambda: to_diag(n).wait_send())
         mir_to_sib(n).wait_send()
-        pl.when(sends_vert(n))(lambda: mir_to_vert(n).wait_send())
-        pl.when(has_down)(lambda: vert_to_sib(n).wait_send())
-        pl.when(sends_turned(n))(lambda: diag_to_mir(n).wait_send())
+        pl.when(has_up)(lambda: pick_to_vert(n).wait_send())
         return carry
 
     lax.fori_loop(0, chunks, finish, 0)
+    pl.when(has_down)(lambda: want_copy().wait_send())
 
     scale = 1.0 / math.sqrt(freqs * windows)
     flip = jnp.where(band_row + band_col == HALF - 1, 1.0, 0.0).astype(jnp.bfloat16)
@@ -263,8 +263,11 @@
             pltpu.VMEM((2, CHUNK, HALF), jnp.float32),
             pltpu.VMEM((2, CHUNK, HALF), jnp.bfloat16),
             pltpu.VMEM((2, stations * stations, HALF), jnp.float32),
-            pltpu.SemaphoreType.DMA((chunks, 7)),
-            pltpu.SemaphoreType.DMA((chunks, 6)),
+            pltpu.VMEM((8, 128), jnp.float32),
+            pltpu.VMEM((8, 128), jnp.float32),
+            pltpu.SemaphoreType.DMA((chunks, 5)),
+            pltpu.SemaphoreType.DMA((chunks, 5)),
+            pltpu.SemaphoreType.DMA((2,)),
         ],
         compiler_params=pltpu.CompilerParams(
             collective_id=0, has_side_effects=True, vmem_limit_bytes=40 * 1024 * 1024),

time: 48.2 us -> 44 us (0.913)
  the two profiles are of different devices: /device:TPU:9 before, /device:TPU:4 now
where the time goes in v2:
time: 44 us; the launch traced here: 43.9 us
  Pallas kernels  39.8 us (90%)
  local copies, waits for them, and re-layouts  3.43 us (8%)
  between operations  0.67 us (2%)
    pallas_call x1, Pallas kernels, local(): pl.pallas_call(functools.partial(kernel, sta, windows, freqs), out_shape=...  39.8 us
    unnamed x4, local copies, waits for them, and re-layouts  3.43 us

profile of v2, /device:TPU:4, one launch (start us, length us, event | category | flops | bytes accessed | tf_op | source)
XLA Modules:
  0.0 43.9 jit_solution(8040914542125542263)
XLA Ops:
  0.7 1.8 %copy.4 = bf16[1,32,4,2,2048]{4,1,3,2,0:T(8,128)(2,1)S(1)} copy(bf16[1,32,4,2,2048]{4,3,2,1,0:T(2,128)(2,1)} %param.3) | data formatting | bytes 2097152 | tf_op args[0]
  2.5 0.0 copy-start
  2.5 0.6 %copy-done = s32[1,2]{1,0:T(1,128)S(1)} copy-done((s32[1,2]{1,0:T(1,128)S(1)}, s32[1,2]{1,0:T(1,128)}, u32[]{:S(2)}) %copy-start) | copy-done | bytes 32
  3.1 39.8 %shard_map.37 = bf16[1024,512]{1,0:T(8,128)(2,1)S(1)} custom-call(s32[1]{0:T(128)S(6)} %copy.6.counts, s32[1,2]{1,0:T(1,128)S(1)} %copy-done, bf16[8,32,2048]{2,1,0:T(8,128)(2,1)S(1)} %bitcast.5), custom_call_target="tpu_custom_call" | custom-call | tf_op jit(solution)/shard_map/pallas_call | solution.py:248
  42.9 1.0 %copy.7 = bf16[1,32,32,512]{3,2,1,0:T(8,128)(2,1)} copy(bf16[1,32,32,512]{3,2,1,0:T(8,128)(2,1)S(1)} %bitcast.4) | data formatting | bytes 2097152
Async XLA Ops:
  2.5 0.7 %copy-start = (s32[1,2]{1,0:T(1,128)S(1)}, s32[1,2]{1,0:T(1,128)}, u32[]{:S(2)}) copy-start(s32[1,2]{1,0:T(1,128)} %pairs.1) | copy-start | bytes 28

commit v3 on v2

--- a/solution.py
+++ b/solution.py
@@ -87,7 +87,7 @@
     band_col = lax.broadcasted_iota(jnp.int32, (CHUNK, CHUNK), 1)
     same_band = jnp.where(
         jnp.right_shift(band_row, 5) == jnp.right_shift(band_col, 5), 1.0 / (BAND * windows), 0.0
-    ).astype(jnp.float32)
+    ).astype(jnp.bfloat16)
 
     def whiten(n):
         cols = pl.ds(pl.multiple_of(n * CHUNK, CHUNK), CHUNK)
@@ -95,7 +95,10 @@
         for part in range(parts):
             value = x_ref[part, :, cols].astype(jnp.float32)
             power += value * value
-        mean = jnp.dot(power, same_band, precision=lax.Precision.HIGHEST, preferred_element_type=jnp.float32)
+        high = power.astype(jnp.bfloat16)
+        low = (power - high.astype(jnp.float32)).astype(jnp.bfloat16)
+        mean = jnp.dot(high, same_band, preferred_element_type=jnp.float32)
+        mean += jnp.dot(low, same_band, preferred_element_type=jnp.float32)
         weight = lax.rsqrt(mean + EPSILON) * mask
         for part in range(parts):
             value = x_ref[part, :, cols].astype(jnp.float32)
@@ -125,9 +128,15 @@
         phase = jnp.where(phase >= period // 2, phase - period, phase)
         return (math.pi / (2 * freqs)) * phase.astype(jnp.float32)
 
-    base_angle = angle_of(band_row * (2 * band_col + 1))
-    base[0] = jnp.cos(base_angle)
-    base[1] = jnp.sin(base_angle)
+    coarse = lax.broadcasted_iota(jnp.int32, (16, HALF), 0)
+    twice = 2 * lax.broadcasted_iota(jnp.int32, (16, HALF), 1) + 1
+    coarse_angle, fine_angle = angle_of(16 * coarse * twice), angle_of(coarse * twice)
+    coarse_cos, coarse_sin = jnp.cos(coarse_angle), jnp.sin(coarse_angle)
+    fine_cos, fine_sin = jnp.cos(fine_angle), jnp.sin(fine_angle)
+    for a in range(CHUNK // 16):
+        cos_a, sin_a = coarse_cos[a:a + 1], coarse_sin[a:a + 1]
+        base[0, a * 16:a * 16 + 16] = cos_a * fine_cos - sin_a * fine_sin
+        base[1, a * 16:a * 16 + 16] = sin_a * fine_cos + cos_a * fine_sin
     acc[...] = jnp.zeros_like(acc)
 
     from_vert = jnp.where(upper == 1, wanted >= 4 * plane + 4, wanted < 4 * plane)
@@ -195,6 +204,16 @@
         def _():
             start_own(n + AHEAD)
 
+        @pl.when(n < chunks)
+        def _():
+            to_sib(n).wait_recv()
+            mir_to_sib(n).wait_recv()
+
+            @pl.when(has_up)
+            def _():
+                pick(n)
+                pick_to_vert(n).start()
+
         @pl.when(n >= 2)
         def _():
             m = n - 2
@@ -202,15 +221,6 @@
             pl.when(has_down)(lambda: pick_to_vert(m).wait_recv())
             compute(m)
 
-        @pl.when(n < chunks)
-        def _():
-            to_sib(n).wait_recv()
-            mir_to_sib(n).wait_recv()
-
-            @pl.when(has_up)
-            def _():
-                pick(n)
-                pick_to_vert(n).start()
         return carry
 
     lax.fori_loop(0, chunks + 2, one_step, 0)

time: 44 us -> 42.7 us (0.970)
  the two profiles are of different devices: /device:TPU:4 before, /device:TPU:0 now
where the time goes in v3:
time: 42.7 us; the launch traced here: 42.6 us
  Pallas kernels  38.5 us (90%)
  local copies, waits for them, and re-layouts  3.43 us (8%)
  between operations  0.67 us (2%)
    pallas_call x1, Pallas kernels, local(): pl.pallas_call(functools.partial(kernel, sta, windows, freqs), out_shape=...  38.5 us
    unnamed x4, local copies, waits for them, and re-layouts  3.43 us

profile of v3, /device:TPU:0, one launch (start us, length us, event | category | flops | bytes accessed | tf_op | source)
XLA Modules:
  0.0 42.6 jit_solution(953027404200177456)
XLA Ops:
  0.7 1.8 %copy.4 = bf16[1,32,4,2,2048]{4,1,3,2,0:T(8,128)(2,1)S(1)} copy(bf16[1,32,4,2,2048]{4,3,2,1,0:T(2,128)(2,1)} %param.3) | data formatting | bytes 2097152 | tf_op args[0]
  2.5 0.0 copy-start
  2.5 0.6 %copy-done = s32[1,2]{1,0:T(1,128)S(1)} copy-done((s32[1,2]{1,0:T(1,128)S(1)}, s32[1,2]{1,0:T(1,128)}, u32[]{:S(2)}) %copy-start) | copy-done | bytes 32
  3.1 38.5 %shard_map.37 = bf16[1024,512]{1,0:T(8,128)(2,1)S(1)} custom-call(s32[1]{0:T(128)S(6)} %copy.6.counts, s32[1,2]{1,0:T(1,128)S(1)} %copy-done, bf16[8,32,2048]{2,1,0:T(8,128)(2,1)S(1)} %bitcast.5), custom_call_target="tpu_custom_call" | custom-call | tf_op jit(solution)/shard_map/pallas_call | solution.py:258
  41.6 1.0 %copy.7 = bf16[1,32,32,512]{3,2,1,0:T(8,128)(2,1)} copy(bf16[1,32,32,512]{3,2,1,0:T(8,128)(2,1)S(1)} %bitcast.4) | data formatting | bytes 2097152
Async XLA Ops:
  2.5 0.7 %copy-start = (s32[1,2]{1,0:T(1,128)S(1)}, s32[1,2]{1,0:T(1,128)}, u32[]{:S(2)}) copy-start(s32[1,2]{1,0:T(1,128)} %pairs.1) | copy-start | bytes 28

commit v4 on v3

--- a/solution.py
+++ b/solution.py
@@ -155,26 +155,33 @@
         for w in range(windows):
             real = held[n, OWN, 2 * w].astype(jnp.float32)
             imag = held[n, OWN, 2 * w + 1].astype(jnp.float32)
-            left[2 * w] = real * turn_cos + imag * turn_sin
-            left[2 * w + 1] = imag * turn_cos - real * turn_sin
+            turned_real = real * turn_cos + imag * turn_sin
+            turned_imag = imag * turn_cos - real * turn_sin
+            left[2 * w] = turned_real
+            left[2 * w + 1] = turned_imag
+            left[parts + w] = turned_real + turned_imag
         for part in range(parts):
             value = held[n, OWN, part]
             for kind, is_it in found:
                 value = jnp.where(is_it, held[n, kind, part], value)
             right[part] = value.astype(jnp.float32)
+        for w in range(windows):
+            right[parts + w] = right[2 * w] - right[2 * w + 1]
 
         def some_rows(g, carry):
             for u in range(8):
                 i = g * 8 + u
-                re = jnp.zeros((32, CHUNK), jnp.float32)
-                im = jnp.zeros((32, CHUNK), jnp.float32)
+                both_re = both_im = mixed = None
                 for w in range(windows):
                     lr = left[2 * w, pl.ds(i, 1), :]
                     li = left[2 * w + 1, pl.ds(i, 1), :]
-                    rr = right[2 * w]
-                    ri = right[2 * w + 1]
-                    re += lr * rr + li * ri
-                    im += li * rr - lr * ri
+                    ls = left[parts + w, pl.ds(i, 1), :]
+                    a, b, c = lr * right[2 * w], li * right[2 * w + 1], ls * right[parts + w]
+                    both_re = a if w == 0 else both_re + a
+                    both_im = b if w == 0 else both_im + b
+                    mixed = c if w == 0 else mixed + c
+                re = both_re + both_im
+                im = mixed - both_re + both_im
                 rows_re[u * 32:(u + 1) * 32] = re.astype(jnp.bfloat16)
                 rows_im[u * 32:(u + 1) * 32] = im.astype(jnp.bfloat16)
             where = pl.ds(pl.multiple_of(g * 256, 256), 256)
@@ -266,8 +273,8 @@
         out_specs=pl.BlockSpec(memory_space=pltpu.VMEM),
         scratch_shapes=[
             pltpu.VMEM((chunks, 7, parts, stations, CHUNK), jnp.bfloat16),
-            pltpu.VMEM((parts, stations, CHUNK), jnp.float32),
-            pltpu.VMEM((parts, stations, CHUNK), jnp.float32),
+            pltpu.VMEM((parts + windows, stations, CHUNK), jnp.float32),
+            pltpu.VMEM((parts + windows, stations, CHUNK), jnp.float32),
             pltpu.VMEM((256, CHUNK), jnp.bfloat16),
             pltpu.VMEM((256, CHUNK), jnp.bfloat16),
             pltpu.VMEM((2, CHUNK, HALF), jnp.float32),

time: 42.7 us -> 42.3 us (level)
  Pallas kernels: 38.5 us -> 38 us
    pallas_call x1, Pallas kernels: 38.5 us -> 38 us  [local(): pl.pallas_call(functools.partial(kernel, sta, windows, freqs), out_shape=...]
where the time goes in v4:
time: 42.3 us; the launch traced here: 42.1 us
  Pallas kernels  38 us (90%)
  local copies, waits for them, and re-layouts  3.43 us (8%)
  between operations  0.67 us (2%)
    pallas_call x1, Pallas kernels, local(): pl.pallas_call(functools.partial(kernel, sta, windows, freqs), out_shape=...  38 us
    unnamed x4, local copies, waits for them, and re-layouts  3.43 us

profile of v4, /device:TPU:0, one launch (start us, length us, event | category | flops | bytes accessed | tf_op | source)
XLA Modules:
  0.0 42.1 jit_solution(5484178540643356637)
XLA Ops:
  0.7 1.8 %copy.4 = bf16[1,32,4,2,2048]{4,1,3,2,0:T(8,128)(2,1)S(1)} copy(bf16[1,32,4,2,2048]{4,3,2,1,0:T(2,128)(2,1)} %param.3) | data formatting | bytes 2097152 | tf_op args[0]
  2.5 0.0 copy-start
  2.5 0.6 %copy-done = s32[1,2]{1,0:T(1,128)S(1)} copy-done((s32[1,2]{1,0:T(1,128)S(1)}, s32[1,2]{1,0:T(1,128)}, u32[]{:S(2)}) %copy-start) | copy-done | bytes 32
  3.1 38.0 %shard_map.37 = bf16[1024,512]{1,0:T(8,128)(2,1)S(1)} custom-call(s32[1]{0:T(128)S(6)} %copy.6.counts, s32[1,2]{1,0:T(1,128)S(1)} %copy-done, bf16[8,32,2048]{2,1,0:T(8,128)(2,1)S(1)} %bitcast.5), custom_call_target="tpu_custom_call" | custom-call | tf_op jit(solution)/shard_map/pallas_call | solution.py:265
  41.2 1.0 %copy.7 = bf16[1,32,32,512]{3,2,1,0:T(8,128)(2,1)} copy(bf16[1,32,32,512]{3,2,1,0:T(8,128)(2,1)S(1)} %bitcast.4) | data formatting | bytes 2097152
Async XLA Ops:
  2.5 0.7 %copy-start = (s32[1,2]{1,0:T(1,128)S(1)}, s32[1,2]{1,0:T(1,128)}, u32[]{:S(2)}) copy-start(s32[1,2]{1,0:T(1,128)} %pairs.1) | copy-start | bytes 28
